TPU v7x, 32 devices: a whole 2x2x4 slice. The times are simulated.
32 devices in a mesh: seq: 8 (over z, y), chan: 4 (over x, core).
Axes of the slice: x: 2, y: 2, z: 4, core: 2. Of those that a mesh axis runs over, the one named last changes fastest.
Arguments:
- stream: bfloat16 [2048, 4096], P('seq', 'chan'), may hold values from -60 to 60
- norm_gain: float32 [4096], P('chan'), may hold values from 0.1 to 1.9
- gate_query: bfloat16 [2048, 4096], P('seq', 'chan'), may hold values from -6 to 6
- gate_key: bfloat16 [2048, 4096], P('seq', 'chan'), may hold values from -6 to 6
- gate_out: bfloat16 [2048, 4096], P('seq', 'chan'), may hold values from -6 to 6
- cotangent: bfloat16 [2048, 4096], P('seq', 'chan'), may hold values from -6 to 6
- medium_filter: float32 [128, 4096], P(None, 'chan'), may hold values from -0.53033009 to 0.53033009
- long_residue: float32 [4096], P('chan'), may hold values from 0.5 to 1.5
- long_rate: float32 [4096], P('chan'), may hold values from 0.000146484375 to 0.0333333333
Outputs:
- grad_query: bfloat16 [2048, 4096], P('seq', 'chan')
- grad_stream: bfloat16 [2048, 4096], P('seq', 'chan')
- grad_filter: float32 [128, 4096], P(None, 'chan')
- grad_residue: float32 [4096], P('chan')
All inputs are finite; a program needn't handle non-finite values.
Results may differ from a plain program's by a relative error of at most 0.008.
Values sent between devices are 32-bit elements; how exact they have to be, the bound alone decides.
A program may use at most 64 MiB of HBM per device.

v0:
```python
import functools

import jax
import jax.numpy as jnp
import ml_dtypes
import numpy as np
from jax import lax
from jax.experimental import pallas as pl
from jax.experimental.pallas import tpu as pltpu
from jax.sharding import PartitionSpec as P

EPSILON = 1e-05
F32 = jnp.float32
BF16 = jnp.bfloat16
MESH = pl.DeviceIdType.MESH
WIDE = 256


def split_np(matrix):
    high = matrix.astype(ml_dtypes.bfloat16)
    low = (matrix - high.astype(np.float64)).astype(ml_dtypes.bfloat16)
    return np.stack([high, low])


def transforms(rows, taps):
    length = rows + taps
    freqs = np.arange(length // 2)[:, None] * 2 + 1
    turns = (freqs * np.arange(length)[None, :]) % (2 * length)
    angle = np.pi * turns / length
    forward = np.concatenate([np.cos(angle), -np.sin(angle)], axis=0)
    inverse = forward.T * (2.0 / length)
    lags = inverse[taps - np.arange(taps)]
    return split_np(forward), split_np(inverse), split_np(lags)


def halves(value):
    high = value.astype(BF16)
    low = (value - high.astype(F32)).astype(BF16)
    return high, low


def product3(mat_ref, rows, cols, value):
    high, low = halves(value)
    mat_high = mat_ref[0, rows, cols]
    mat_low = mat_ref[1, rows, cols]
    total = jnp.dot(mat_high, high, preferred_element_type=F32)
    total += jnp.dot(mat_low, high, preferred_element_type=F32)
    return total + jnp.dot(mat_high, low, preferred_element_type=F32)


def kernel(
    n,
    m,
    stream_hbm,
    gain_hbm,
    query_hbm,
    key_hbm,
    gate_out_hbm,
    cotangent_hbm,
    taps_hbm,
    residue_hbm,
    rate_hbm,
    fwd_hbm,
    inv_hbm,
    lag_hbm,
    out_query,
    out_stream,
    out_filter,
    out_residue,
    stream,
    gain,
    query,
    key,
    gate_out,
    cotangent,
    taps_ref,
    residue,
    rate,
    fwd,
    inv,
    lag,
    raw,
    entering,
    rev,
    gm,
    raw_halo,
    gm_halo,
    inv_col,
    row_send,
    row_recv,
    inv_halo,
    carry_send,
    carry_recv,
    fh,
    xh,
    gh,
    gf,
    rs_recv,
    part,
    ex_recv,
    ag,
    res_all,
    weighted,
    load_sem,
    inv_sem,
    halo_sem,
    gm_sem,
    row_sem,
    carry_sem,
    rs_sem,
    ex_sem,
    ag_sem,
    res_sem,
):
    s, c = lax.axis_index("seq"), lax.axis_index("chan")
    R, C = stream.shape
    K = taps_ref.shape[0]
    N = R + K
    H = N // 2
    T, A, chunk, _ = gf.shape
    B = n // A
    a, b = lax.div(s, B), lax.rem(s, B)
    channel_total = C * m
    token_total = R * n
    head, tail = pl.ds(0, R - K), pl.ds(R - K, K)

    loads = {}

    def load(name, src, dst):
        loads[name] = pltpu.make_async_copy(src, dst, load_sem.at[len(loads)])
        loads[name].start()

    load("gain", gain_hbm, gain)
    load("stream_tail", stream_hbm.at[tail, :], stream.at[tail, :])
    load("key_tail", key_hbm.at[tail, :], key.at[tail, :])
    load("stream_head", stream_hbm.at[head, :], stream.at[head, :])
    load("key_head", key_hbm.at[head, :], key.at[head, :])
    load("rate", rate_hbm, rate)
    load("gate_out", gate_out_hbm, gate_out)
    load("cotangent", cotangent_hbm, cotangent)
    load("fwd", fwd_hbm, fwd)
    load("taps", taps_hbm, taps_ref)
    load("residue", residue_hbm, residue)
    load("query", query_hbm, query)
    load("lag", lag_hbm, lag)
    load("inv", inv_hbm, inv)

    barrier = pltpu.get_barrier_semaphore()

    def greet(d, _):
        pl.semaphore_signal(barrier, inc=1, device_id=(lax.rem(s + d, n), c), device_id_type=MESH)
        return 0

    lax.fori_loop(1, n, greet, 0)
    for d in range(1, m):
        pl.semaphore_signal(barrier, inc=1, device_id=(s, lax.rem(c + d, m)), device_id_type=MESH)

    def tiles(width, step, init=0):
        def run(i, carry):
            return step(i, pl.ds(pl.multiple_of(i * width, width), width), carry)

        return lax.fori_loop(0, C // width, run, init)

    def lanes(value):
        return sum(value[:, i * 128 : (i + 1) * 128] for i in range(value.shape[1] // 128))

    def wide(col):
        return jnp.concatenate([col] * (WIDE // 128), axis=1)

    def to_row(acc):
        return jnp.broadcast_to(jnp.sum(acc.T, axis=0, keepdims=True), (8, R))

    def to_col(row):
        return jnp.broadcast_to(row[0:1, :], (128, R)).T

    def copy(src, dst, sems, index, target):
        return pltpu.make_async_remote_copy(
            src_ref=src,
            dst_ref=dst,
            send_sem=sems.at[0, index],
            recv_sem=sems.at[1, index],
            device_id=target,
            device_id_type=MESH,
        )

    after = (lax.rem(s + 1, n), c)
    before = (lax.rem(s + n - 1, n), c)

    def halo_copy(i, cols):
        return copy(raw.at[tail, cols], raw_halo.at[:, cols], halo_sem, i, after)

    def gm_copy(i, cols):
        return copy(gm.at[pl.ds(0, K), cols], gm_halo.at[:, cols], gm_sem, i, before)

    inv_copy = copy(row_send.at[2], inv_halo, inv_sem, 0, after)

    def row_copy(kind, d):
        return copy(
            row_send.at[kind],
            row_recv.at[kind, d - 1],
            row_sem,
            kind * (m - 1) + d - 1,
            (s, lax.rem(c + d, m)),
        )

    def gated(rows, cols, acc):
        x = stream[rows, cols].astype(F32)
        raw[rows, cols] = key[rows, cols].astype(F32) * x * gain[:, cols]
        return acc + lanes(x * x)

    loads["gain"].wait()
    loads["stream_tail"].wait()
    loads["key_tail"].wait()
    squares_tail = tiles(
        WIDE, lambda i, cols, acc: gated(tail, cols, acc), jnp.zeros((K, 128), F32)
    )
    pl.semaphore_wait(barrier, n - 1 + m - 1)

    @pl.when(s < n - 1)
    def _():
        def start(i, cols, _):
            halo_copy(i, cols).start()
            return 0

        tiles(WIDE, start)

    loads["stream_head"].wait()
    loads["key_head"].wait()
    squares_head = tiles(
        WIDE, lambda i, cols, acc: gated(head, cols, acc), jnp.zeros((R - K, 128), F32)
    )
    squares = to_row(jnp.concatenate([squares_head, squares_tail], axis=0))
    row_send[0] = squares
    for d in range(1, m):
        row_copy(0, d).start()

    loads["rate"].wait()
    loads["gate_out"].wait()
    loads["cotangent"].wait()

    def recur(i, cols, _):
        value = gate_out[:, cols].astype(F32) * cotangent[:, cols].astype(F32)
        slow = rate[:, cols]
        row = lax.broadcasted_iota(jnp.int32, value.shape, 0)
        k = 1
        while k < R:
            factor = jnp.exp(-slow * k)
            if k < 8:
                moved = jnp.where(row < R - k, pltpu.roll(value, R - k, 0), 0.0)
            else:
                moved = jnp.concatenate([value[k:], jnp.zeros((k, value.shape[1]), F32)], axis=0)
            value = value + factor * moved
            k *= 2
        rev[:, cols] = value
        carry_send[:, cols] = value[0:1]
        return 0

    tiles(128, recur)

    def carry_copy(d):
        return copy(
            carry_send, carry_recv.at[d - 1], carry_sem, d - 1, (lax.rem(s + n - d, n), c)
        )

    def start_carry(d, _):
        carry_copy(d).start()
        return 0

    lax.fori_loop(1, s + 1, start_carry, 0)

    loads["fwd"].wait()
    loads["taps"].wait()

    def tap_spectrum(i, cols, _):
        fh[:, cols] = product3(fwd, slice(None), slice(0, K), taps_ref[:, cols])
        return 0

    tiles(WIDE, tap_spectrum)

    loads["residue"].wait()
    loads["query"].wait()

    def wait_carry(d, _):
        carry_copy(d).wait_recv()
        return 0

    lax.fori_loop(1, n - s, wait_carry, 0)
    block_decay = jnp.exp(-rate[...] * R)

    def horner(i, later):
        return block_decay * later + carry_recv[n - 2 - s - i]

    entering[...] = lax.fori_loop(0, n - 1 - s, horner, jnp.zeros((1, C), F32))

    def norm_factor(slow):
        z = 2.0 * slow
        poly = 1.0 - z / 6.0
        for k in (5.0, 4.0, 3.0, 2.0):
            poly = 1.0 - z / k * poly
        return jnp.sqrt(z * poly)

    def state(i, cols, _):
        slow = rate[:, cols]
        position = lax.broadcasted_iota(jnp.int32, (R, WIDE), 0).astype(F32)
        value = rev[:, cols] + jnp.exp(-slow * (R - position)) * entering[:, cols]
        rev[:, cols] = value
        gm[:, cols] = query[:, cols].astype(F32) * (residue[:, cols] * norm_factor(slow) * value)

        @pl.when(s > 0)
        def _():
            gm_copy(i, cols).start()

        return 0

    tiles(WIDE, state)

    total = squares
    for d in range(1, m):
        row_copy(0, d).wait_recv()
        total = total + row_recv[0, d - 1]
    inv_row = lax.rsqrt(total / channel_total + EPSILON)
    row_send[2] = inv_row
    inv_col[...] = to_col(inv_row)

    @pl.when(s < n - 1)
    def _():
        inv_copy.start()

    def local_spectra(i, cols, _):
        gh[:, cols] = product3(fwd, slice(None), slice(0, R), gm[:, cols])
        value = raw[:, cols] * wide(inv_col[...])
        xh[:, cols] = product3(fwd, slice(None), slice(K, N), value)
        return 0

    tiles(WIDE, local_spectra)

    @pl.when(s > 0)
    def _():
        inv_copy.wait_recv()

    loads["lag"].wait()
    loads["inv"].wait()

    def at_line(d):
        return (lax.rem(a + d, A) * B + b, c)

    def rs_copy(i, d):
        return copy(
            gf.at[i, lax.rem(a + d, A)],
            rs_recv.at[i, d - 1],
            rs_sem,
            i * (A - 1) + d - 1,
            at_line(d),
        )

    def forward(i, cols, _):
        @pl.when(s > 0)
        def _():
            halo_copy(i, cols).wait_recv()
            halo = raw_halo[:, cols] * wide(to_col(inv_halo[...])[R - K :])
            xh[:, cols] = xh[:, cols] + product3(fwd, slice(None), slice(0, K), halo)

        xr, xi = xh[:H, cols], xh[H:, cols]
        gr, gi = gh[:H, cols], gh[H:, cols]
        spectrum = jnp.concatenate([gr * xr + gi * xi, gr * xi - gi * xr], axis=0)
        value = product3(lag, slice(None), slice(None), spectrum)
        for k in range(A):
            gf[i, k] = value[k * chunk : (k + 1) * chunk]

        def start(d, _):
            rs_copy(i, d).start()
            return 0

        lax.fori_loop(1, A, start, 0)

        fr, fi = fh[:H, cols], fh[H:, cols]
        spectrum = jnp.concatenate([fr * xr - fi * xi, fr * xi + fi * xr], axis=0)
        mixed = product3(inv, slice(K, N), slice(None), spectrum)
        factor = norm_factor(rate[:, cols])
        states = rev[:, cols]
        out_query[:, cols] = (mixed * (residue[:, cols] * factor * states)).astype(BF16)
        stored = (query[:, cols].astype(F32) * mixed).astype(BF16).astype(F32)
        res_all[s, :, cols] = factor * jnp.sum(stored * states, axis=0, keepdims=True)
        return 0

    tiles(WIDE, forward)

    def res_copy(d):
        return copy(res_all.at[s], res_all.at[s], res_sem, d - 1, (lax.rem(s + d, n), c))

    def start_res(d, _):
        res_copy(d).start()
        return 0

    lax.fori_loop(1, n, start_res, 0)

    def ex_copy(i):
        return copy(part.at[i], ex_recv.at[i], ex_sem, i, (a * B + (B - 1 - b), c))

    def ag_copy(i, d):
        return copy(ag.at[i, a], ag.at[i, a], ag_sem, i * (A - 1) + d - 1, at_line(d))

    def add_line(i, _):
        def add(d, total):
            rs_copy(i, d).wait_recv()
            return total + rs_recv[i, d - 1]

        part[i] = lax.fori_loop(1, A, add, gf[i, a])
        if B == 2:
            ex_copy(i).start()
        return 0

    lax.fori_loop(0, T, add_line, 0)
    scale = token_total**-0.5

    def add_partner(i, _):
        total = part[i]
        if B == 2:
            ex_copy(i).wait_recv()
            total = total + ex_recv[i]
        ag[i, a] = total * scale

        def start(d, _):
            ag_copy(i, d).start()
            return 0

        lax.fori_loop(1, A, start, 0)
        return 0

    lax.fori_loop(0, T, add_partner, 0)

    def backward(i, cols, acc):
        @pl.when(s < n - 1)
        def _():
            gm_copy(i, cols).wait_recv()
            gh[:, cols] = gh[:, cols] + product3(fwd, slice(None), slice(R, N), gm_halo[:, cols])

        gr, gi = gh[:H, cols], gh[H:, cols]
        fr, fi = fh[:H, cols], fh[H:, cols]
        spectrum = jnp.concatenate([fr * gr + fi * gi, fr * gi - fi * gr], axis=0)
        grad = product3(inv, slice(0, R), slice(None), spectrum)
        value = gain[:, cols] * key[:, cols].astype(F32) * grad
        weighted[:, cols] = value
        return acc + lanes(value * stream[:, cols].astype(F32))

    dots = to_row(tiles(WIDE, backward, jnp.zeros((R, 128), F32)))
    row_send[1] = dots
    for d in range(1, m):
        row_copy(1, d).start()
    for d in range(1, m):
        row_copy(1, d).wait_recv()
        dots = dots + row_recv[1, d - 1]
    dots_col = to_col(dots / channel_total)

    def finish(i, cols, _):
        scale_rows = wide(inv_col[...])
        pull = wide(inv_col[...] * inv_col[...] * dots_col)
        value = weighted[:, cols] - stream[:, cols].astype(F32) * pull
        out_stream[:, cols] = (scale_rows * value).astype(BF16)
        return 0

    tiles(WIDE, finish)

    def res_arrived(d, _):
        res_copy(d).wait_recv()
        return 0

    lax.fori_loop(1, n, res_arrived, 0)
    out_residue[...] = (
        lax.fori_loop(0, n, lambda i, total: total + res_all[i], jnp.zeros((1, C), F32)) * scale
    )

    def spread(i, cols, _):
        def arrived(d, _):
            ag_copy(i, d).wait_recv()
            return 0

        lax.fori_loop(1, A, arrived, 0)
        for k in range(A):
            out_filter[k * chunk : (k + 1) * chunk, cols] = ag[i, k]
        return 0

    tiles(WIDE, spread)

    for d in range(1, m):
        row_copy(0, d).wait_send()
        row_copy(1, d).wait_send()

    def left(i, cols, _):
        @pl.when(s < n - 1)
        def _():
            halo_copy(i, cols).wait_send()

        @pl.when(s > 0)
        def _():
            gm_copy(i, cols).wait_send()

        if B == 2:
            ex_copy(i).wait_send()

        def line(d, _):
            rs_copy(i, d).wait_send()
            ag_copy(i, d).wait_send()
            return 0

        lax.fori_loop(1, A, line, 0)
        return 0

    tiles(WIDE, left)

    @pl.when(s < n - 1)
    def _():
        inv_copy.wait_send()

    def carry_sent(d, _):
        carry_copy(d).wait_send()
        return 0

    lax.fori_loop(1, s + 1, carry_sent, 0)

    def res_sent(d, _):
        res_copy(d).wait_send()
        return 0

    lax.fori_loop(1, n, res_sent, 0)


def solution(mesh):
    n, m = mesh.shape["seq"], mesh.shape["chan"]

    def body(
        stream,
        norm_gain,
        gate_query,
        gate_key,
        gate_out,
        cotangent,
        medium_filter,
        long_residue,
        long_rate,
    ):
        R, C = stream.shape
        K = medium_filter.shape[0]
        N = R + K
        mats = [jnp.asarray(mat) for mat in transforms(R, K)]
        T = C // WIDE
        B = 2 if n % 2 == 0 else 1
        A = n // B
        vmem = pl.BlockSpec(memory_space=pltpu.VMEM)
        hbm = pl.BlockSpec(memory_space=pltpu.HBM)

        def buffer(*shape):
            return pltpu.VMEM(shape, F32)

        def sems(count):
            return pltpu.SemaphoreType.DMA((2, count))

        outs = pl.pallas_call(
            functools.partial(kernel, n, m),
            out_shape=(
                jax.ShapeDtypeStruct((R, C), BF16),
                jax.ShapeDtypeStruct((R, C), BF16),
                jax.ShapeDtypeStruct((K, C), F32),
                jax.ShapeDtypeStruct((1, C), F32),
            ),
            in_specs=[hbm] * 12,
            out_specs=(vmem,) * 4,
            scratch_shapes=[
                pltpu.VMEM((R, C), BF16),
                buffer(1, C),
                pltpu.VMEM((R, C), BF16),
                pltpu.VMEM((R, C), BF16),
                pltpu.VMEM((R, C), BF16),
                pltpu.VMEM((R, C), BF16),
                buffer(K, C),
                buffer(1, C),
                buffer(1, C),
                *(pltpu.VMEM(mat.shape, BF16) for mat in mats),
                buffer(R, C),
                buffer(1, C),
                buffer(R, C),
                buffer(R, C),
                buffer(K, C),
                buffer(K, C),
                buffer(R, 128),
                buffer(3, 8, R),
                buffer(2, m - 1, 8, R),
                buffer(8, R),
                buffer(1, C),
                buffer(n - 1, 1, C),
                buffer(N, C),
                buffer(N, C),
                buffer(N, C),
                buffer(T, A, K // A, WIDE),
                buffer(T, A - 1, K // A, WIDE),
                buffer(T, K // A, WIDE),
                buffer(T, K // A, WIDE),
                buffer(T, A, K // A, WIDE),
                buffer(n, 1, C),
                buffer(R, C),
                pltpu.SemaphoreType.DMA((14,)),
                sems(1),
                sems(T),
                sems(T),
                sems(2 * (m - 1)),
                sems(n - 1),
                sems(T * (A - 1)),
                sems(T),
                sems(T * (A - 1)),
                sems(n - 1),
            ],
            compiler_params=pltpu.CompilerParams(
                collective_id=0, has_side_effects=True, vmem_limit_bytes=48 * 2**20
            ),
            cost_estimate=pl.CostEstimate(
                flops=2 * (2 * N + 2 * R + 2 * K) * N * C * 3,
                bytes_accessed=8 * R * C * 2,
                transcendentals=R * C,
            ),
        )(
            stream,
            norm_gain[None],
            gate_query,
            gate_key,
            gate_out,
            cotangent,
            medium_filter,
            long_residue[None],
            long_rate[None],
            *mats,
        )
        return outs[0], outs[1], outs[2], outs[3][0]

    in_specs = (
        P("seq", "chan"),
        P("chan"),
        P("seq", "chan"),
        P("seq", "chan"),
        P("seq", "chan"),
        P("seq", "chan"),
        P(None, "chan"),
        P("chan"),
        P("chan"),
    )
    out_specs = (P("seq", "chan"), P("seq", "chan"), P(None, "chan"), P("chan"))
    return jax.shard_map(body, mesh=mesh, in_specs=in_specs, out_specs=out_specs, check_vma=False)
```

profile of v0, /device:TPU:0, one launch (start us, length us, event | category | flops | bytes accessed | tf_op | source)
XLA Modules:
  0.0 74.7 jit_solution(7213120960360875482)
XLA Ops:
  0.6 0.0 copy-start.6
  0.6 0.7 copy-done.6
  1.3 0.0 copy-start
  1.3 1.0 %copy-done = bf16[256,1024]{1,0:T(8,128)(2,1)S(1)} copy-done((bf16[256,1024]{1,0:T(8,128)(2,1)S(1)}, bf16[256,1024]{1,0:T(8,128)(2,1)}, u32[]{:S(2)}) %copy-start) | copy-done | bytes 524312
  2.4 0.0 copy-start.1
  2.4 1.0 %copy-done.1 = bf16[256,1024]{1,0:T(8,128)(2,1)S(1)} copy-done((bf16[256,1024]{1,0:T(8,128)(2,1)S(1)}, bf16[256,1024]{1,0:T(8,128)(2,1)}, u32[]{:S(2)}) %copy-start.1) | copy-done | bytes 524312
  3.4 0.0 copy-start.2
  3.4 1.0 %copy-done.2 = bf16[256,1024]{1,0:T(8,128)(2,1)S(1)} copy-done((bf16[256,1024]{1,0:T(8,128)(2,1)S(1)}, bf16[256,1024]{1,0:T(8,128)(2,1)}, u32[]{:S(2)}) %copy-start.2) | copy-done | bytes 524312
  4.4 0.0 copy-start.3
  4.5 1.0 %copy-done.3 = bf16[256,1024]{1,0:T(8,128)(2,1)S(1)} copy-done((bf16[256,1024]{1,0:T(8,128)(2,1)S(1)}, bf16[256,1024]{1,0:T(8,128)(2,1)}, u32[]{:S(2)}) %copy-start.3) | copy-done | bytes 524312
  5.5 0.0 copy-start.4
  5.5 1.0 %copy-done.4 = bf16[256,1024]{1,0:T(8,128)(2,1)S(1)} copy-done((bf16[256,1024]{1,0:T(8,128)(2,1)S(1)}, bf16[256,1024]{1,0:T(8,128)(2,1)}, u32[]{:S(2)}) %copy-start.4) | copy-done | bytes 524312
  6.5 0.0 copy-start.5
  6.5 1.0 %copy-done.5 = f32[128,1024]{1,0:T(8,128)S(1)} copy-done((f32[128,1024]{1,0:T(8,128)S(1)}, f32[128,1024]{1,0:T(8,128)}, u32[]{:S(2)}) %copy-start.5) | copy-done | bytes 524312
  7.6 0.0 copy-start.7
  7.6 0.7 copy-done.7
  8.3 0.0 copy-start.8
  8.3 0.7 copy-done.8
  8.9 0.0 copy-start.9
  9.0 1.1 %copy-done.9 = bf16[2,384,384]{2,1,0:T(8,128)(2,1)S(1)} copy-done((bf16[2,384,384]{2,1,0:T(8,128)(2,1)S(1)}, bf16[2,384,384]{2,1,0:T(8,128)(2,1)}, u32[]{:S(2)}) %copy-start.9) | copy-done | bytes 589848
  10.0 0.0 copy-start.10
  10.0 1.1 %copy-done.10 = bf16[2,384,384]{2,1,0:T(8,128)(2,1)S(1)} copy-done((bf16[2,384,384]{2,1,0:T(8,128)(2,1)S(1)}, bf16[2,384,384]{2,1,0:T(8,128)(2,1)}, u32[]{:S(2)}) %copy-start.10) | copy-done | bytes 589848
  11.1 0.0 copy-start.11
  11.1 0.9 %copy-done.11 = bf16[2,128,384]{2,1,0:T(8,128)(2,1)S(1)} copy-done((bf16[2,128,384]{2,1,0:T(8,128)(2,1)S(1)}, bf16[2,128,384]{2,1,0:T(8,128)(2,1)}, u32[]{:S(2)}) %copy-start.11) | copy-done | bytes 196632
  12.0 59.8 %shard_map.147 = (bf16[256,1024]{1,0:T(8,128)(2,1)S(1)}, bf16[256,1024]{1,0:T(8,128)(2,1)S(1)}, f32[128,1024]{1,0:T(8,128)S(1)}, f32[1,1024]{1,0:T(1,128)S(1)}) custom-call(bf16[256,1024]{1,0:T(8,128)(2,1)S(1)} %copy-done, f32[1,1024]{1,0:T(1,128)S(1)} %bitcast.5, bf16[256,1024]{1,0:T(8,128)(2,1)S(1)} %copy-done.1, bf16[256,1024]{1,0:T(8,128)(2,1)S(1)} %copy-done.2, ...), custom_call_target="tpu_custom_call" | custom-call | flops 3623878656 | bytes 4194304 | tf_op jit(solution)/shard_map/pallas_call | solution.py:558
  71.8 0.8 %copy.20 = bf16[256,1024]{1,0:T(8,128)(2,1)} copy(bf16[256,1024]{1,0:T(8,128)(2,1)S(1)} %get-tuple-element.16) | data formatting | bytes 1048576
  72.6 0.8 %copy.21 = bf16[256,1024]{1,0:T(8,128)(2,1)} copy(bf16[256,1024]{1,0:T(8,128)(2,1)S(1)} %get-tuple-element.17) | data formatting | bytes 1048576
  73.4 0.8 %copy.22 = f32[128,1024]{1,0:T(8,128)} copy(f32[128,1024]{1,0:T(8,128)S(1)} %get-tuple-element.18) | data formatting | bytes 1048576
  74.2 0.6 copy.23
Async XLA Ops:
  0.6 0.7 copy-start.6
  1.3 1.0 %copy-start = (bf16[256,1024]{1,0:T(8,128)(2,1)S(1)}, bf16[256,1024]{1,0:T(8,128)(2,1)}, u32[]{:S(2)}) copy-start(bf16[256,1024]{1,0:T(8,128)(2,1)} %stream_hbm.1) | copy-start | bytes 1572868
  2.4 1.0 %copy-start.1 = (bf16[256,1024]{1,0:T(8,128)(2,1)S(1)}, bf16[256,1024]{1,0:T(8,128)(2,1)}, u32[]{:S(2)}) copy-start(bf16[256,1024]{1,0:T(8,128)(2,1)} %query_hbm.1) | copy-start | bytes 1572868
  3.4 1.0 %copy-start.2 = (bf16[256,1024]{1,0:T(8,128)(2,1)S(1)}, bf16[256,1024]{1,0:T(8,128)(2,1)}, u32[]{:S(2)}) copy-start(bf16[256,1024]{1,0:T(8,128)(2,1)} %key_hbm.1) | copy-start | bytes 1572868
  4.4 1.0 %copy-start.3 = (bf16[256,1024]{1,0:T(8,128)(2,1)S(1)}, bf16[256,1024]{1,0:T(8,128)(2,1)}, u32[]{:S(2)}) copy-start(bf16[256,1024]{1,0:T(8,128)(2,1)} %gate_out_hbm.1) | copy-start | bytes 1572868
  5.5 1.0 %copy-start.4 = (bf16[256,1024]{1,0:T(8,128)(2,1)S(1)}, bf16[256,1024]{1,0:T(8,128)(2,1)}, u32[]{:S(2)}) copy-start(bf16[256,1024]{1,0:T(8,128)(2,1)} %cotangent_hbm.1) | copy-start | bytes 1572868
  6.5 1.0 %copy-start.5 = (f32[128,1024]{1,0:T(8,128)S(1)}, f32[128,1024]{1,0:T(8,128)}, u32[]{:S(2)}) copy-start(f32[128,1024]{1,0:T(8,128)} %taps_hbm.1) | copy-start | bytes 1572868
  7.6 0.7 copy-start.7
  8.3 0.7 copy-start.8
  8.9 1.1 %copy-start.9 = (bf16[2,384,384]{2,1,0:T(8,128)(2,1)S(1)}, bf16[2,384,384]{2,1,0:T(8,128)(2,1)}, u32[]{:S(2)}) copy-start(bf16[2,384,384]{2,1,0:T(8,128)(2,1)} %constant.7.clone.inv_hbm) | copy-start | bytes 1769476
  10.0 1.1 %copy-start.10 = (bf16[2,384,384]{2,1,0:T(8,128)(2,1)S(1)}, bf16[2,384,384]{2,1,0:T(8,128)(2,1)}, u32[]{:S(2)}) copy-start(bf16[2,384,384]{2,1,0:T(8,128)(2,1)} %constant.6.clone.fwd_hbm) | copy-start | bytes 1769476
  11.1 0.9 %copy-start.11 = (bf16[2,128,384]{2,1,0:T(8,128)(2,1)S(1)}, bf16[2,128,384]{2,1,0:T(8,128)(2,1)}, u32[]{:S(2)}) copy-start(bf16[2,128,384]{2,1,0:T(8,128)(2,1)} %constant.8.clone.lag_hbm) | copy-start | bytes 589828
where the time goes:
time: 75.5 us; the launch traced here: 74.7 us
  Pallas kernels  59.8 us (79%)
  local copies, waits for them, and re-layouts  14.3 us (19%)
    pallas_call x1, Pallas kernels, body(): pl.pallas_call(functools.partial(kernel, n, m), out_shape=(jax.ShapeDtype...  59.8 us
    unnamed x28, local copies, waits for them, and re-layouts  14.3 us

commit v1 on v0

--- a/solution.py
+++ b/solution.py
@@ -305,11 +305,6 @@
         value = rev[:, cols] + jnp.exp(-slow * (R - position)) * entering[:, cols]
         rev[:, cols] = value
         gm[:, cols] = query[:, cols].astype(F32) * (residue[:, cols] * norm_factor(slow) * value)
-
-        @pl.when(s > 0)
-        def _():
-            gm_copy(i, cols).start()
-
         return 0
 
     tiles(WIDE, state)
@@ -372,6 +367,10 @@
             return 0
 
         lax.fori_loop(1, A, start, 0)
+
+        @pl.when(s > 0)
+        def _():
+            gm_copy(i, cols).start()
 
         fr, fi = fh[:H, cols], fh[H:, cols]
         spectrum = jnp.concatenate([fr * xr - fi * xi, fr * xi + fi * xr], axis=0)
@@ -610,7 +609,7 @@
                 sems(n - 1),
             ],
             compiler_params=pltpu.CompilerParams(
-                collective_id=0, has_side_effects=True, vmem_limit_bytes=48 * 2**20
+                collective_id=0, has_side_effects=True, vmem_limit_bytes=62 * 2**20
             ),
             cost_estimate=pl.CostEstimate(
                 flops=2 * (2 * N + 2 * R + 2 * K) * N * C * 3,

time: 75.5 us -> 62.6 us (0.83)
  local copies, waits for them, and re-layouts: 14.3 us -> 4.55 us
  Pallas kernels: 59.8 us -> 57.2 us
    unnamed x28 -> x10, local copies, waits for them, and re-layouts: 14.3 us -> 4.55 us
    pallas_call x1, Pallas kernels: 59.8 us -> 57.2 us  [body(): pl.pallas_call(functools.partial(kernel, n, m), out_shape=(jax.ShapeDtype...]
where the time goes in v1:
time: 62.6 us; the launch traced here: 62.4 us
  Pallas kernels  57.2 us (91%)
  local copies, waits for them, and re-layouts  4.55 us (7%)
  between operations  0.65 us (1%)
    pallas_call x1, Pallas kernels, body(): pl.pallas_call(functools.partial(kernel, n, m), out_shape=(jax.ShapeDtype...  57.2 us
    unnamed x10, local copies, waits for them, and re-layouts  4.55 us

profile of v1, /device:TPU:0, one launch (start us, length us, event | category | flops | bytes accessed | tf_op | source)
XLA Modules:
  0.0 62.4 jit_solution(16131119155177745386)
XLA Ops:
  0.6 57.2 %shard_map.147 = (bf16[256,1024]{1,0:T(8,128)(2,1)}, bf16[256,1024]{1,0:T(8,128)(2,1)}, f32[128,1024]{1,0:T(8,128)}, f32[1,1024]{1,0:T(1,128)}) custom-call(bf16[256,1024]{1,0:T(8,128)(2,1)} %stream_hbm.1, f32[1,1024]{1,0:T(1,128)} %bitcast.5, bf16[256,1024]{1,0:T(8,128)(2,1)} %query_hbm.1, bf16[256,1024]{1,0:T(8,128)(2,1)} %key_hbm.1, ...), custom_call_target="tpu_custom_call" | custom-call | flops 3623878656 | bytes 4194304 | tf_op jit(solution)/shard_map/pallas_call | solution.py:557
  57.9 0.0 copy-start.1
  57.9 1.9 %copy.20 = bf16[256,1024]{1,0:T(8,128)(2,1)} copy(bf16[256,1024]{1,0:T(8,128)(2,1)} %get-tuple-element.16) | data formatting | bytes 1048576
  59.8 0.0 copy-done.1
  59.8 0.0 copy-start
  59.8 0.8 %copy.21 = bf16[256,1024]{1,0:T(8,128)(2,1)} copy(bf16[256,1024]{1,0:T(8,128)(2,1)S(1)} %copy-done.1) | data formatting | bytes 1048576
  60.6 0.4 copy-done
  61.0 0.0 copy-start.2
  61.0 0.8 %copy.22 = f32[128,1024]{1,0:T(8,128)} copy(f32[128,1024]{1,0:T(8,128)S(1)} %copy-done) | data formatting | bytes 1048576
  61.8 0.0 copy-done.2
  61.8 0.6 copy.23
Async XLA Ops:
  57.9 1.9 %copy-start.1 = (bf16[256,1024]{1,0:T(8,128)(2,1)S(1)}, bf16[256,1024]{1,0:T(8,128)(2,1)}, u32[]{:S(2)}) copy-start(bf16[256,1024]{1,0:T(8,128)(2,1)} %get-tuple-element.17) | copy-start | bytes 1572868
  59.8 1.2 %copy-start = (f32[128,1024]{1,0:T(8,128)S(1)}, f32[128,1024]{1,0:T(8,128)}, u32[]{:S(2)}) copy-start(f32[128,1024]{1,0:T(8,128)} %get-tuple-element.18) | copy-start | bytes 1572868
  61.0 0.8 %copy-start.2 = (f32[1,1024]{1,0:T(1,128)S(1)}, f32[1,1024]{1,0:T(1,128)}, u32[]{:S(2)}) copy-start(f32[1,1024]{1,0:T(1,128)} %get-tuple-element.11) | copy-start | bytes 12292

commit v2 on v1

--- a/solution.py
+++ b/solution.py
@@ -110,6 +110,7 @@
     rs_sem,
     ex_sem,
     ag_sem,
+    fwd_sem,
     res_sem,
 ):
     s, c = lax.axis_index("seq"), lax.axis_index("chan")
@@ -405,25 +406,34 @@
             return total + rs_recv[i, d - 1]
 
         part[i] = lax.fori_loop(1, A, add, gf[i, a])
-        if B == 2:
+
+        @pl.when(lax.rem(i, B) != b)
+        def _():
             ex_copy(i).start()
+
         return 0
 
     lax.fori_loop(0, T, add_line, 0)
     scale = token_total**-0.5
 
+    def fwd_copy(i):
+        return copy(ag.at[i], ag.at[i], fwd_sem, i, (a * B + (B - 1 - b), c))
+
     def add_partner(i, _):
-        total = part[i]
-        if B == 2:
-            ex_copy(i).wait_recv()
-            total = total + ex_recv[i]
-        ag[i, a] = total * scale
-
-        def start(d, _):
-            ag_copy(i, d).start()
-            return 0
-
-        lax.fori_loop(1, A, start, 0)
+        @pl.when(lax.rem(i, B) == b)
+        def _():
+            total = part[i]
+            if B == 2:
+                ex_copy(i).wait_recv()
+                total = total + ex_recv[i]
+            ag[i, a] = total * scale
+
+            def start(d, _):
+                ag_copy(i, d).start()
+                return 0
+
+            lax.fori_loop(1, A, start, 0)
+
         return 0
 
     lax.fori_loop(0, T, add_partner, 0)
@@ -446,6 +456,21 @@
     row_send[1] = dots
     for d in range(1, m):
         row_copy(1, d).start()
+
+    def gathered(i, _):
+        @pl.when(lax.rem(i, B) == b)
+        def _():
+            def arrived(d, _):
+                ag_copy(i, d).wait_recv()
+                return 0
+
+            lax.fori_loop(1, A, arrived, 0)
+            if B == 2:
+                fwd_copy(i).start()
+
+        return 0
+
+    lax.fori_loop(0, T, gathered, 0)
     for d in range(1, m):
         row_copy(1, d).wait_recv()
         dots = dots + row_recv[1, d - 1]
@@ -470,11 +495,10 @@
     )
 
     def spread(i, cols, _):
-        def arrived(d, _):
-            ag_copy(i, d).wait_recv()
-            return 0
-
-        lax.fori_loop(1, A, arrived, 0)
+        @pl.when(lax.rem(i, B) != b)
+        def _():
+            fwd_copy(i).wait_recv()
+
         for k in range(A):
             out_filter[k * chunk : (k + 1) * chunk, cols] = ag[i, k]
         return 0
@@ -494,15 +518,26 @@
         def _():
             gm_copy(i, cols).wait_send()
 
-        if B == 2:
-            ex_copy(i).wait_send()
-
         def line(d, _):
             rs_copy(i, d).wait_send()
-            ag_copy(i, d).wait_send()
             return 0
 
         lax.fori_loop(1, A, line, 0)
+
+        @pl.when(lax.rem(i, B) != b)
+        def _():
+            ex_copy(i).wait_send()
+
+        @pl.when(lax.rem(i, B) == b)
+        def _():
+            def line(d, _):
+                ag_copy(i, d).wait_send()
+                return 0
+
+            lax.fori_loop(1, A, line, 0)
+            if B == 2:
+                fwd_copy(i).wait_send()
+
         return 0
 
     tiles(WIDE, left)
@@ -522,6 +557,15 @@
         return 0
 
     lax.fori_loop(1, n, res_sent, 0)
+
+
+def hand_over(*refs):
+    sem = refs[8]
+    copies = [pltpu.make_async_copy(refs[i], refs[4 + i], sem.at[i]) for i in range(4)]
+    for one in copies:
+        one.start()
+    for one in copies:
+        one.wait()
 
 
 def solution(mesh):
@@ -606,6 +650,7 @@
                 sems(T * (A - 1)),
                 sems(T),
                 sems(T * (A - 1)),
+                sems(T),
                 sems(n - 1),
             ],
             compiler_params=pltpu.CompilerParams(
@@ -628,6 +673,14 @@
             long_rate[None],
             *mats,
         )
+        outs = pl.pallas_call(
+            hand_over,
+            out_shape=tuple(jax.ShapeDtypeStruct(out.shape, out.dtype) for out in outs),
+            in_specs=[hbm] * 4,
+            out_specs=(hbm,) * 4,
+            scratch_shapes=[pltpu.SemaphoreType.DMA((4,))],
+            compiler_params=pltpu.CompilerParams(vmem_limit_bytes=62 * 2**20),
+        )(*outs)
         return outs[0], outs[1], outs[2], outs[3][0]
 
     in_specs = (

time: 62.6 us -> 106 us (1.69)
  Pallas kernels: 57.2 us -> 104 us
  local copies, waits for them, and re-layouts: 4.55 us -> 0 us
    pallas_call x0 -> x1, Pallas kernels: none -> 48.9 us  [body(): pl.pallas_call(hand_over, out_shape=tuple((jax.ShapeDtypeStruct(out.shape...]
    unnamed x10 -> x0, local copies, waits for them, and re-layouts: 4.55 us -> none
    pallas_call x1, Pallas kernels: 57.2 us -> 55.3 us  [body(): pl.pallas_call(functools.partial(kernel, n, m), out_shape=(jax.ShapeDtype...]
where the time goes in v2:
time: 106 us; the launch traced here: 105 us
  Pallas kernels  104 us (98%)
    pallas_call x1, Pallas kernels, body(): pl.pallas_call(functools.partial(kernel, n, m), out_shape=(jax.ShapeDtype...  55.3 us
    pallas_call x1, Pallas kernels, body(): pl.pallas_call(hand_over, out_shape=tuple((jax.ShapeDtypeStruct(out.shape...  48.9 us

profile of v2, /device:TPU:0, one launch (start us, length us, event | category | flops | bytes accessed | tf_op | source)
XLA Modules:
  0.0 104.9 jit_solution(2734818563306214747)
XLA Ops:
  0.6 55.3 %shard_map.147 = (bf16[256,1024]{1,0:T(8,128)(2,1)}, bf16[256,1024]{1,0:T(8,128)(2,1)}, f32[128,1024]{1,0:T(8,128)}, f32[1,1024]{1,0:T(1,128)}) custom-call(bf16[256,1024]{1,0:T(8,128)(2,1)} %stream_hbm.1, f32[1,1024]{1,0:T(1,128)} %bitcast.4, bf16[256,1024]{1,0:T(8,128)(2,1)} %query_hbm.1, bf16[256,1024]{1,0:T(8,128)(2,1)} %key_hbm.1, ...), custom_call_target="tpu_custom_call" | custom-call | flops 3623878656 | bytes 4194304 | tf_op jit(solution)/shard_map/pallas_call | solution.py:601
  56.0 48.9 %shard_map.148 = (bf16[256,1024]{1,0:T(8,128)(2,1)}, bf16[256,1024]{1,0:T(8,128)(2,1)}, f32[128,1024]{1,0:T(8,128)}, f32[1,1024]{1,0:T(1,128)}) custom-call(bf16[256,1024]{1,0:T(8,128)(2,1)} %get-tuple-element.12.refs_0_, bf16[256,1024]{1,0:T(8,128)(2,1)} %get-tuple-element.13.refs_1_, f32[128,1024]{1,0:T(8,128)} %get-tuple-element.14.refs_2_, ...), custom_call_target="tpu_custom_call" | custom-call | tf_op jit(solution)/shard_map/pallas_call | solution.py:676

commit v3 on v2

--- a/solution.py
+++ b/solution.py
@@ -33,19 +33,10 @@
     return split_np(forward), split_np(inverse), split_np(lags)
 
 
-def halves(value):
-    high = value.astype(BF16)
-    low = (value - high.astype(F32)).astype(BF16)
-    return high, low
-
-
-def product3(mat_ref, rows, cols, value):
-    high, low = halves(value)
-    mat_high = mat_ref[0, rows, cols]
-    mat_low = mat_ref[1, rows, cols]
-    total = jnp.dot(mat_high, high, preferred_element_type=F32)
-    total += jnp.dot(mat_low, high, preferred_element_type=F32)
-    return total + jnp.dot(mat_high, low, preferred_element_type=F32)
+def product2(mat_ref, rows, cols, value):
+    value = value.astype(BF16)
+    total = jnp.dot(mat_ref[0, rows, cols], value, preferred_element_type=F32)
+    return total + jnp.dot(mat_ref[1, rows, cols], value, preferred_element_type=F32)
 
 
 def kernel(
@@ -273,7 +264,7 @@
     loads["taps"].wait()
 
     def tap_spectrum(i, cols, _):
-        fh[:, cols] = product3(fwd, slice(None), slice(0, K), taps_ref[:, cols])
+        fh[:, cols] = product2(fwd, slice(None), slice(0, K), taps_ref[:, cols])
         return 0
 
     tiles(WIDE, tap_spectrum)
@@ -323,9 +314,9 @@
         inv_copy.start()
 
     def local_spectra(i, cols, _):
-        gh[:, cols] = product3(fwd, slice(None), slice(0, R), gm[:, cols])
+        gh[:, cols] = product2(fwd, slice(None), slice(0, R), gm[:, cols])
         value = raw[:, cols] * wide(inv_col[...])
-        xh[:, cols] = product3(fwd, slice(None), slice(K, N), value)
+        xh[:, cols] = product2(fwd, slice(None), slice(K, N), value)
         return 0
 
     tiles(WIDE, local_spectra)
@@ -354,12 +345,12 @@
         def _():
             halo_copy(i, cols).wait_recv()
             halo = raw_halo[:, cols] * wide(to_col(inv_halo[...])[R - K :])
-            xh[:, cols] = xh[:, cols] + product3(fwd, slice(None), slice(0, K), halo)
+            xh[:, cols] = xh[:, cols] + product2(fwd, slice(None), slice(0, K), halo)
 
         xr, xi = xh[:H, cols], xh[H:, cols]
         gr, gi = gh[:H, cols], gh[H:, cols]
         spectrum = jnp.concatenate([gr * xr + gi * xi, gr * xi - gi * xr], axis=0)
-        value = product3(lag, slice(None), slice(None), spectrum)
+        value = product2(lag, slice(None), slice(None), spectrum)
         for k in range(A):
             gf[i, k] = value[k * chunk : (k + 1) * chunk]
 
@@ -375,7 +366,7 @@
 
         fr, fi = fh[:H, cols], fh[H:, cols]
         spectrum = jnp.concatenate([fr * xr - fi * xi, fr * xi + fi * xr], axis=0)
-        mixed = product3(inv, slice(K, N), slice(None), spectrum)
+        mixed = product2(inv, slice(K, N), slice(None), spectrum)
         factor = norm_factor(rate[:, cols])
         states = rev[:, cols]
         out_query[:, cols] = (mixed * (residue[:, cols] * factor * states)).astype(BF16)
@@ -442,12 +433,12 @@
         @pl.when(s < n - 1)
         def _():
             gm_copy(i, cols).wait_recv()
-            gh[:, cols] = gh[:, cols] + product3(fwd, slice(None), slice(R, N), gm_halo[:, cols])
+            gh[:, cols] = gh[:, cols] + product2(fwd, slice(None), slice(R, N), gm_halo[:, cols])
 
         gr, gi = gh[:H, cols], gh[H:, cols]
         fr, fi = fh[:H, cols], fh[H:, cols]
         spectrum = jnp.concatenate([fr * gr + fi * gi, fr * gi - fi * gr], axis=0)
-        grad = product3(inv, slice(0, R), slice(None), spectrum)
+        grad = product2(inv, slice(0, R), slice(None), spectrum)
         value = gain[:, cols] * key[:, cols].astype(F32) * grad
         weighted[:, cols] = value
         return acc + lanes(value * stream[:, cols].astype(F32))
@@ -560,11 +551,15 @@
 
 
 def hand_over(*refs):
-    sem = refs[8]
-    copies = [pltpu.make_async_copy(refs[i], refs[4 + i], sem.at[i]) for i in range(4)]
-    for one in copies:
+    held, sem = refs[8:12], refs[12]
+    into = [pltpu.make_async_copy(refs[i], held[i], sem.at[0, i]) for i in range(4)]
+    away = [pltpu.make_async_copy(held[i], refs[4 + i], sem.at[1, i]) for i in range(4)]
+    for one in into:
         one.start()
-    for one in copies:
+    for first, second in zip(into, away):
+        first.wait()
+        second.start()
+    for one in away:
         one.wait()
 
 
@@ -657,7 +652,7 @@
                 collective_id=0, has_side_effects=True, vmem_limit_bytes=62 * 2**20
             ),
             cost_estimate=pl.CostEstimate(
-                flops=2 * (2 * N + 2 * R + 2 * K) * N * C * 3,
+                flops=2 * (2 * N + 2 * R + 2 * K) * N * C * 2,
                 bytes_accessed=8 * R * C * 2,
                 transcendentals=R * C,
             ),
@@ -678,7 +673,10 @@
             out_shape=tuple(jax.ShapeDtypeStruct(out.shape, out.dtype) for out in outs),
             in_specs=[hbm] * 4,
             out_specs=(hbm,) * 4,
-            scratch_shapes=[pltpu.SemaphoreType.DMA((4,))],
+            scratch_shapes=[
+                *(pltpu.VMEM(out.shape, out.dtype) for out in outs),
+                pltpu.SemaphoreType.DMA((2, 4)),
+            ],
             compiler_params=pltpu.CompilerParams(vmem_limit_bytes=62 * 2**20),
         )(*outs)
         return outs[0], outs[1], outs[2], outs[3][0]

time: 106 us -> 58.2 us (0.55)
  Pallas kernels: 104 us -> 56.9 us
    pallas_call x1, Pallas kernels: 48.9 us -> 2.25 us  [body(): pl.pallas_call(hand_over, out_shape=tuple((jax.ShapeDtypeStruct(out.shape...]
where the time goes in v3:
time: 58.2 us; the launch traced here: 57.6 us
  Pallas kernels  56.9 us (98%)
  between operations  0.64 us (1%)
    pallas_call x1, Pallas kernels, body(): pl.pallas_call(functools.partial(kernel, n, m), out_shape=(jax.ShapeDtype...  54.7 us
    pallas_call x1, Pallas kernels, body(): pl.pallas_call(hand_over, out_shape=tuple((jax.ShapeDtypeStruct(out.shape...  2.25 us

profile of v3, /device:TPU:0, one launch (start us, length us, event | category | flops | bytes accessed | tf_op | source)
XLA Modules:
  0.0 57.6 jit_solution(10961220193979082717)
XLA Ops:
  0.6 54.7 %shard_map.147 = (bf16[256,1024]{1,0:T(8,128)(2,1)}, bf16[256,1024]{1,0:T(8,128)(2,1)}, f32[128,1024]{1,0:T(8,128)}, f32[1,1024]{1,0:T(1,128)}) custom-call(bf16[256,1024]{1,0:T(8,128)(2,1)} %stream_hbm.1, f32[1,1024]{1,0:T(1,128)} %bitcast.4, bf16[256,1024]{1,0:T(8,128)(2,1)} %query_hbm.1, bf16[256,1024]{1,0:T(8,128)(2,1)} %key_hbm.1, ...), custom_call_target="tpu_custom_call" | custom-call | flops 2415919104 | bytes 4194304 | tf_op jit(solution)/shard_map/pallas_call | solution.py:596
  55.3 2.3 %shard_map.148 = (bf16[256,1024]{1,0:T(8,128)(2,1)}, bf16[256,1024]{1,0:T(8,128)(2,1)}, f32[128,1024]{1,0:T(8,128)}, f32[1,1024]{1,0:T(1,128)}) custom-call(bf16[256,1024]{1,0:T(8,128)(2,1)} %get-tuple-element.12.refs_0_, bf16[256,1024]{1,0:T(8,128)(2,1)} %get-tuple-element.13.refs_1_, f32[128,1024]{1,0:T(8,128)} %get-tuple-element.14.refs_2_, ...), custom_call_target="tpu_custom_call" | custom-call | tf_op jit(solution)/shard_map/pallas_call | solution.py:671

commit v4 on v3

--- a/solution.py
+++ b/solution.py
@@ -297,6 +297,11 @@
         value = rev[:, cols] + jnp.exp(-slow * (R - position)) * entering[:, cols]
         rev[:, cols] = value
         gm[:, cols] = query[:, cols].astype(F32) * (residue[:, cols] * norm_factor(slow) * value)
+
+        @pl.when((s > 0) & (lax.rem(c, 2) == 0))
+        def _():
+            gm_copy(i, cols).start()
+
         return 0
 
     tiles(WIDE, state)
@@ -360,10 +365,6 @@
 
         lax.fori_loop(1, A, start, 0)
 
-        @pl.when(s > 0)
-        def _():
-            gm_copy(i, cols).start()
-
         fr, fi = fh[:H, cols], fh[H:, cols]
         spectrum = jnp.concatenate([fr * xr - fi * xi, fr * xi + fi * xr], axis=0)
         mixed = product2(inv, slice(K, N), slice(None), spectrum)
@@ -375,6 +376,14 @@
         return 0
 
     tiles(WIDE, forward)
+
+    @pl.when((s > 0) & (lax.rem(c, 2) == 1))
+    def _():
+        def start(i, cols, _):
+            gm_copy(i, cols).start()
+            return 0
+
+        tiles(WIDE, start)
 
     def res_copy(d):
         return copy(res_all.at[s], res_all.at[s], res_sem, d - 1, (lax.rem(s + d, n), c))

time: 58.2 us -> 56.9 us (0.978)
  Pallas kernels: 56.9 us -> 56.1 us
    pallas_call x1, Pallas kernels: 54.7 us -> 53.8 us  [body(): pl.pallas_call(functools.partial(kernel, n, m), out_shape=(jax.ShapeDtype...]
where the time goes in v4:
time: 56.9 us; the launch traced here: 56.7 us
  Pallas kernels  56.1 us (99%)
  between operations  0.64 us (1%)
    pallas_call x1, Pallas kernels, body(): pl.pallas_call(functools.partial(kernel, n, m), out_shape=(jax.ShapeDtype...  53.8 us
    pallas_call x1, Pallas kernels, body(): pl.pallas_call(hand_over, out_shape=tuple((jax.ShapeDtypeStruct(out.shape...  2.25 us

profile of v4, /device:TPU:0, one launch (start us, length us, event | category | flops | bytes accessed | tf_op | source)
XLA Modules:
  0.0 56.7 jit_solution(1866234035127173216)
XLA Ops:
  0.6 53.8 %shard_map.147 = (bf16[256,1024]{1,0:T(8,128)(2,1)}, bf16[256,1024]{1,0:T(8,128)(2,1)}, f32[128,1024]{1,0:T(8,128)}, f32[1,1024]{1,0:T(1,128)}) custom-call(bf16[256,1024]{1,0:T(8,128)(2,1)} %stream_hbm.1, f32[1,1024]{1,0:T(1,128)} %bitcast.4, bf16[256,1024]{1,0:T(8,128)(2,1)} %query_hbm.1, bf16[256,1024]{1,0:T(8,128)(2,1)} %key_hbm.1, ...), custom_call_target="tpu_custom_call" | custom-call | flops 2415919104 | bytes 4194304 | tf_op jit(solution)/shard_map/pallas_call | solution.py:605
  54.4 2.3 %shard_map.148 = (bf16[256,1024]{1,0:T(8,128)(2,1)}, bf16[256,1024]{1,0:T(8,128)(2,1)}, f32[128,1024]{1,0:T(8,128)}, f32[1,1024]{1,0:T(1,128)}) custom-call(bf16[256,1024]{1,0:T(8,128)(2,1)} %get-tuple-element.12.refs_0_, bf16[256,1024]{1,0:T(8,128)(2,1)} %get-tuple-element.13.refs_1_, f32[128,1024]{1,0:T(8,128)} %get-tuple-element.14.refs_2_, ...), custom_call_target="tpu_custom_call" | custom-call | tf_op jit(solution)/shard_map/pallas_call | solution.py:680
